TPU v7x, 32 devices: a whole 2x2x4 slice. The times are simulated.
32 devices in a mesh: row: 8 (over z, y), col: 4 (over x, core).
Axes of the slice: x: 2, y: 2, z: 4, core: 2. Of those that a mesh axis runs over, the one named last changes fastest.
Arguments:
- sources: bfloat16 [32768, 128], P(('col', 'row')), may hold values from -6 to 6
- adjoint_sources: bfloat16 [32768, 128], P(('row', 'col')), may hold values from -6 to 6
- points: float32 [2, 32768], replicated, may hold values from 0 to 40
- element_of: int32 [32768], replicated, may hold values from 0 to 127
- wavenumbers: float32 [128], replicated, may hold values from 1.5 to 4
- quad_weight: float32 [32768], replicated, may hold values from 0.01 to 0.04
- near_leaves: int32 [8, 4, 2, 24], P('row', 'col'), may hold values from 0 to 15, as said below
- helper_slot: int32 [8, 4, 24], P('row', 'col'), may hold values from -1 to 11, as said below
- far_leaves: int32 [8, 4, 2, 32], P('row', 'col'), may hold values from 0 to 15, as said below
- far_rank: int32 [8, 4, 32], P('row', 'col'), may hold values from 16 to 64
- far_left: bfloat16 [8, 4, 32, 512, 128], P('row', 'col'), may hold values from -0.125 to 0.125
- far_right: bfloat16 [8, 4, 32, 512, 128], P('row', 'col'), may hold values from -0.1875 to 0.1875
Outputs:
- field: float32 [32768, 128], P(('row', 'col'))
- adjoint_field: float32 [32768, 128], P(('col', 'row'))
Inputs may be any that keep to these rules, and one draw needn't show every extreme that they name: `near_leaves`: entry [r, c, 0, t] is a row leaf within row segment r (below 8) and entry [r, c, 1, t] a column leaf within column segment c (below 16); in one block of the partition all near and far pairs are distinct. `far_leaves`: as for near_leaves: row leaves below 8, column leaves below 16, and no pair of a block repeats a near or far pair of that block. Task slot t of block (r, c) belongs to the helper at row index t // 3 with the same col index. Within one col index, each pair (helper, helper_slot) is used by at most one task, so a helper takes at most 12 tasks; in every col index some block has all 24 slots live.
All inputs are finite; a program needn't handle non-finite values.
Results may differ from a plain program's by a relative error of at most 0.0031.
Values may be sent and summed in bfloat16 or wider, within the bound.
A program may use at most 128 MiB of HBM per device.

v0:
```python
import math

import jax
import jax.numpy as jnp
from jax import lax
from jax.experimental import pallas as pl
from jax.experimental.pallas import tpu as pltpu
from jax.sharding import PartitionSpec as P

LEAF = 512
RMAX = 64
LANES = 128
CHUNK = 64

DAMPING = 0.02
SOFTENING = 0.01

SIN_TERMS = (4.4428679821848505, -7.307445410211019, 3.5948020760296724, -0.7844035523165803)
COS_TERMS = (
    1.4142134965678808,
    -6.978850988354271,
    5.7394611717976725,
    -1.8835629903422064,
    0.31069819203200194,
)
ROUNDER = 12582912.0


def polynomial(terms, value):
    total = terms[-1]
    for term in terms[-2::-1]:
        total = total * value + term
    return total


def rotate(panel):
    half = panel.shape[-1] // 2
    return jnp.concatenate([-panel[..., half:], panel[..., :half]], axis=-1)


def rotate_rows(panel):
    half = panel.shape[-2] // 2
    return jnp.concatenate([-panel[..., half:, :], panel[..., :half, :]], axis=-2)


def params():
    return pltpu.CompilerParams(vmem_limit_bytes=52 * 1024 * 1024)


def tile_kernel(
    rows_ref,
    cols_ref,
    live_ref,
    place_ref,
    row_points,
    col_points,
    kinds,
    weights,
    waves,
    tile_ref,
    row_wide,
    col_info,
):
    task = pl.program_id(0)

    @pl.when(task == 0)
    def _():
        def widen(leaf, carry):
            span = pl.ds(pl.multiple_of(leaf * LEAF, LEAF), LEAF)
            for axis in range(2):
                line = row_points[axis : axis + 1, span]
                row_wide[axis, leaf] = jnp.broadcast_to(line, (LANES, LEAF)).T
            return carry

        lax.fori_loop(0, row_wide.shape[1], widen, 0)

        def gather(leaf, carry):
            span = pl.ds(pl.multiple_of(leaf * LEAF, LEAF), LEAF)
            count = waves.shape[0]
            ids = lax.broadcasted_iota(jnp.int32, (count, LEAF), 0)
            chosen = jnp.where(ids == kinds[:, span], waves[...], 0.0)
            col_info[leaf, 0:1] = col_points[0:1, span]
            col_info[leaf, 1:2] = col_points[1:2, span]
            col_info[leaf, 2:3] = jnp.sum(chosen, axis=0, keepdims=True)
            col_info[leaf, 3:4] = weights[:, span]
            return carry

        lax.fori_loop(0, col_info.shape[0], gather, 0)

    @pl.when(live_ref[task] > 0)
    def _():
        row = rows_ref[task]
        col = cols_ref[task]
        for lane in range(LEAF // LANES):
            span = slice(lane * LANES, (lane + 1) * LANES)
            col_x = col_info[col, 0:1, span]
            col_y = col_info[col, 1:2, span]
            col_turns = col_info[col, 2:3, span]
            col_weight = col_info[col, 3:4, span]

            def chunk(step, carry):
                rows = pl.ds(pl.multiple_of(step * CHUNK, CHUNK), CHUNK)
                delta_x = row_wide[0, row, rows, :] - col_x
                delta_y = row_wide[1, row, rows, :] - col_y
                radius_sq = delta_x * delta_x + delta_y * delta_y
                radius = radius_sq * lax.rsqrt(jnp.maximum(radius_sq, 1e-30))
                softened = radius_sq + SOFTENING
                fourth = lax.rsqrt(softened * lax.rsqrt(softened))
                decay = jnp.exp2(radius * (-DAMPING * math.log2(math.e)))
                amplitude = (col_weight * decay) * fourth
                turns = radius * col_turns
                part = turns - ((turns + ROUNDER) - ROUNDER)
                part_sq = part * part
                sine = part * polynomial(SIN_TERMS, part_sq)
                cosine = polynomial(COS_TERMS, part_sq)
                scaled = amplitude * sine
                tile_ref[0, 0, rows, span] = (amplitude - scaled * sine).astype(jnp.bfloat16)
                tile_ref[0, 1, rows, span] = (scaled * cosine).astype(jnp.bfloat16)
                return carry

            lax.fori_loop(0, LEAF // CHUNK, chunk, 0)


def make_tiles(near_rows, near_cols, live, place, points, kinds, weights, waves, row_count, col_count):
    count = near_rows.shape[0]
    return pl.pallas_call(
        tile_kernel,
        out_shape=jax.ShapeDtypeStruct((count, 2, LEAF, LEAF), jnp.bfloat16),
        grid_spec=pltpu.PrefetchScalarGridSpec(
            num_scalar_prefetch=4,
            grid=(count,),
            in_specs=[
                pl.BlockSpec((2, row_count * LEAF), lambda t, r, c, v, p: (0, p[0])),
                pl.BlockSpec((2, col_count * LEAF), lambda t, r, c, v, p: (0, p[1])),
                pl.BlockSpec((1, col_count * LEAF), lambda t, r, c, v, p: (0, p[1])),
                pl.BlockSpec((1, col_count * LEAF), lambda t, r, c, v, p: (0, p[1])),
                pl.BlockSpec(waves.shape, lambda t, r, c, v, p: (0, 0)),
            ],
            out_specs=pl.BlockSpec((1, 2, LEAF, LEAF), lambda t, r, c, v, p: (t, 0, 0, 0)),
            scratch_shapes=[
                pltpu.VMEM((2, row_count, LEAF, LANES), jnp.float32),
                pltpu.VMEM((col_count, 8, LEAF), jnp.float32),
            ],
        ),
        compiler_params=params(),
        cost_estimate=pl.CostEstimate(
            flops=60 * count * LEAF * LEAF * 100, bytes_accessed=count * 4 * LEAF * LEAF, transcendentals=0
        ),
        name="tiles",
    )(near_rows, near_cols, live, place, points, points, kinds, weights, waves)


def dot(left, right, left_dim, right_dim):
    return lax.dot_general(
        left, right, (((left_dim,), (right_dim,)), ((), ())), preferred_element_type=jnp.float32
    )


def core_of(projected, rank, sign):
    swapped = rotate_rows(projected[:, RMAX:])
    core = projected[:, :RMAX] + sign * swapped
    kept = lax.broadcasted_iota(jnp.int32, core.shape, 1) < rank
    core = jnp.where(kept, core, 0.0)
    both = jnp.concatenate([core, sign * rotate_rows(core)], axis=1)
    return both.astype(jnp.bfloat16)


def adjoint_kernel(
    per_step, nr, nc, live, fr, fc, rank, place, tiles, left, right, *rest
):
    *pieces, total, narrow, panel, turned = rest
    step = pl.program_id(0)
    near_per, far_per = per_step

    @pl.when(step == 0)
    def _():
        total[...] = jnp.zeros_like(total)
        leaves = pieces[0].shape[0] // LEAF
        for shift, piece in enumerate(pieces):
            owner = lax.rem(place[1] - shift + len(pieces), len(pieces))
            for local in range(leaves):
                flipped = piece[local * LEAF : (local + 1) * LEAF, :].T
                panel[owner * leaves + local] = flipped
                turned[owner * leaves + local] = -rotate_rows(flipped)

    blocks = [step * far_per + local for local in range(far_per)]
    projected = [dot(panel[fr[b]], left[n], 1, 0) for n, b in enumerate(blocks)]
    tasks = [step * near_per + local for local in range(near_per)]
    near = [
        dot(panel[nr[t]], tiles[n, 0], 1, 0) + dot(turned[nr[t]], tiles[n, 1], 1, 0)
        for n, t in enumerate(tasks)
    ]
    cores = [core_of(projected[n], rank[b], -1.0) for n, b in enumerate(blocks)]
    for n, t in enumerate(tasks):
        total[nc[t]] += jnp.where(live[t] > 0, near[n], 0.0)
    for n, b in enumerate(blocks):
        total[fc[b]] += dot(cores[n], right[n], 1, 1)

    @pl.when(step == pl.num_programs(0) - 1)
    def _():
        narrow[...] = total[...].astype(jnp.bfloat16)


def forward_kernel(
    per_step, nr, nc, live, fr, fc, rank, place, tiles, left, right, source, total, narrow, flat, turned
):
    step = pl.program_id(0)
    near_per, far_per = per_step

    @pl.when(step == 0)
    def _():
        total[...] = jnp.zeros_like(total)

        def prepare(leaf, carry):
            block = source[leaf]
            flat[leaf] = block.T
            turned[leaf] = rotate(block)
            return carry

        lax.fori_loop(0, source.shape[0], prepare, 0)

    blocks = [step * far_per + local for local in range(far_per)]
    projected = [dot(flat[fc[b]], right[n], 1, 0) for n, b in enumerate(blocks)]
    tasks = [step * near_per + local for local in range(near_per)]
    near = [
        dot(tiles[n, 0], source[nc[t]], 1, 0) + dot(tiles[n, 1], turned[nc[t]], 1, 0)
        for n, t in enumerate(tasks)
    ]
    cores = [core_of(projected[n], rank[b], 1.0) for n, b in enumerate(blocks)]
    for n, t in enumerate(tasks):
        product = near[n].astype(jnp.bfloat16).astype(jnp.float32)
        total[nr[t]] += jnp.where(live[t] > 0, product, 0.0)
    for n, b in enumerate(blocks):
        total[fr[b]] += dot(left[n], cores[n], 1, 1)

    @pl.when(step == pl.num_programs(0) - 1)
    def _():
        narrow[...] = total[...].astype(jnp.bfloat16)


def apply_blocks(kernel, name, lists, tiles, panels, left, right, out_shape, scratch):
    near_count = tiles.shape[0]
    far_count = left.shape[0]
    steps = math.gcd(near_count, far_count)
    near_per, far_per = near_count // steps, far_count // steps

    def whole(shape):
        zeros = (0,) * len(shape)
        return pl.BlockSpec(shape, lambda t, *_: zeros)

    factor = pl.BlockSpec((far_per, LEAF, 2 * RMAX), lambda t, *_: (t, 0, 0))

    def body(*refs):
        kernel((near_per, far_per), *refs)

    return pl.pallas_call(
        body,
        out_shape=(
            jax.ShapeDtypeStruct(out_shape, jnp.float32),
            jax.ShapeDtypeStruct(out_shape, jnp.bfloat16),
        ),
        grid_spec=pltpu.PrefetchScalarGridSpec(
            num_scalar_prefetch=7,
            grid=(steps,),
            in_specs=[
                pl.BlockSpec((near_per, 2, LEAF, LEAF), lambda t, *_: (t, 0, 0, 0)),
                factor,
                factor,
                *[whole(panel.shape) for panel in panels],
            ],
            out_specs=(whole(out_shape), whole(out_shape)),
            scratch_shapes=[pltpu.VMEM(shape, jnp.bfloat16) for shape in scratch],
        ),
        compiler_params=params(),
        cost_estimate=pl.CostEstimate(
            flops=near_count * 4 * LEAF * LEAF * LANES * 30, bytes_accessed=near_count * 4 * LEAF * LEAF, transcendentals=0
        ),
        name=name,
    )(*lists, tiles, left, right, *panels)


def scatter_sum(wide, narrow, axis, index, size):
    unit = (wide.shape[0] * wide.shape[1]) // size
    wide = wide.reshape((size, unit) + wide.shape[2:])
    narrow = narrow.reshape((size, unit) + narrow.shape[2:])
    own = lax.dynamic_index_in_dim(wide, index, 0, keepdims=False)
    arrived = []
    for shift in range(1, size):
        target = lax.rem(index + shift, size)
        piece = lax.dynamic_index_in_dim(narrow, target, 0, keepdims=False)
        arrived.append(
            lax.ppermute(piece, axis, [(at, (at + shift) % size) for at in range(size)])
        )
    for piece in arrived:
        own = own + piece.astype(jnp.float32)
    return own


def make_per_device(row_size, col_size):
    def per_device(
        sources,
        adjoint_sources,
        points,
        element_of,
        wavenumbers,
        quad_weight,
        near_leaves,
        helper_slot,
        far_leaves,
        far_rank,
        far_left,
        far_right,
    ):
        row_index = lax.axis_index("row")
        col_index = lax.axis_index("col")
        width = sources.shape[1]
        source_block = lax.all_gather(sources, "row", axis=0, tiled=True)
        adjoint_pieces = [adjoint_sources] + [
            lax.ppermute(
                adjoint_sources, "col", [(at, (at + shift) % col_size) for at in range(col_size)]
            )
            for shift in range(1, col_size)
        ]
        col_count = source_block.shape[0] // LEAF
        row_count = adjoint_sources.shape[0] * col_size // LEAF
        near_rows = near_leaves[0, 0, 0]
        near_cols = near_leaves[0, 0, 1]
        live = (helper_slot[0, 0] >= 0).astype(jnp.int32)
        far_rows = far_leaves[0, 0, 0]
        far_cols = far_leaves[0, 0, 1]
        ranks = far_rank[0, 0]
        left = far_left[0, 0]
        right = far_right[0, 0]

        row_span = row_count * LEAF
        col_span = col_count * LEAF
        place = jnp.stack([row_index, col_index]).astype(jnp.int32)
        tiles = make_tiles(
            near_rows,
            near_cols,
            live,
            place,
            points,
            element_of[None, :],
            quad_weight[None, :],
            jnp.broadcast_to((wavenumbers * (0.5 / math.pi))[:, None], (wavenumbers.shape[0], LEAF)),
            row_count,
            col_count,
        )

        lists = (near_rows, near_cols, live, far_rows, far_cols, ranks, place)
        adjoint_wide, adjoint_narrow = apply_blocks(
            adjoint_kernel,
            "adjoint",
            lists,
            tiles,
            adjoint_pieces,
            left,
            right,
            (col_count, width, LEAF),
            [(row_count, width, LEAF)] * 2,
        )
        adjoint_narrow, tiles = lax.optimization_barrier((adjoint_narrow, tiles))

        field_wide, field_narrow = apply_blocks(
            forward_kernel,
            "forward",
            lists,
            tiles,
            (source_block.reshape(col_count, LEAF, width),),
            left,
            right,
            (row_count, LEAF, width),
            [(col_count, width, LEAF), (col_count, LEAF, width)],
        )

        unit = col_span // row_size
        if unit % LEAF == 0:
            adjoint = scatter_sum(
                adjoint_wide.reshape(row_size, -1, width, LEAF),
                adjoint_narrow.reshape(row_size, -1, width, LEAF),
                "row",
                row_index,
                row_size,
            )
            adjoint_field = adjoint.transpose(0, 2, 1).reshape(unit, width)
        else:
            adjoint = scatter_sum(
                adjoint_wide.transpose(0, 2, 1).reshape(row_size, unit, width),
                adjoint_narrow.transpose(0, 2, 1).reshape(row_size, unit, width),
                "row",
                row_index,
                row_size,
            )
            adjoint_field = adjoint.reshape(unit, width)
        unit = row_span // col_size
        field = scatter_sum(
            field_wide.reshape(col_size, unit, width),
            field_narrow.reshape(col_size, unit, width),
            "col",
            col_index,
            col_size,
        )
        return (field.reshape(unit, width), adjoint_field)

    return per_device


def solution(mesh):
    return jax.shard_map(
        make_per_device(mesh.shape["row"], mesh.shape["col"]),
        mesh=mesh,
        in_specs=(
            P(("col", "row"), None),
            P(("row", "col"), None),
            P(),
            P(),
            P(),
            P(),
            P("row", "col", None, None),
            P("row", "col", None),
            P("row", "col", None, None),
            P("row", "col", None),
            P("row", "col", None, None, None),
            P("row", "col", None, None, None),
        ),
        out_specs=(P(("row", "col"), None), P(("col", "row"), None)),
        check_vma=False,
    )
```

profile of v0, /device:TPU:1, one launch (start us, length us, event | category | flops | bytes accessed | tf_op | source)
XLA Modules:
  0.0 155.8 jit_solution(3381020520522344646)
XLA Ops:
  7.2 0.0 all-gather.2.cloned.1.call-start
  7.2 2.7 %collective-permute-start = (bf16[1024,128]{1,0:T(8,128)(2,1)}, bf16[1024,128]{1,0:T(8,128)(2,1)S(1)}, u32[]{:S(2)}, u32[]{:S(2)}) collective-permute-start(bf16[1024,128]{1,0:T(8,128)(2,1)} %refs_10_.1), channel_id=1, source_target_pairs={{0,1},{1,2},{2,3},{3,0},{4,5},{5,6},{6,7},{7,4},{8,9},{9,10},{10,1... | collective-permute-start | bytes 786440 | tf_op jit(solution)/shard_map/ppermute | solution.py:319
  9.9 0.0 collective-permute-start.1
  9.9 0.5 collective-permute-start.2
  10.3 0.0 all-gather.2.cloned.1.call-update
  10.4 0.8 slice_bitcast_fusion.2
  11.1 0.7 fusion.9.live_ref.refs_2_
  11.8 0.7 broadcast_multiply_fusion
  12.4 0.1 pad_add_fusion.place_ref.refs_6_
  12.5 0.1 broadcast_in_dim.14.waves
  12.6 0.0 copy-start
  12.6 0.9 copy-done
  13.6 0.9 copy-done.2
  14.5 0.9 copy-done.3
  15.4 31.5 %tiles.1.refs_7_ = bf16[24,2,512,512]{3,2,1,0:T(8,128)(2,1)} custom-call(s32[24]{0:T(128)S(1)} %get-tuple-element.27.rows_ref.refs_0_, s32[24]{0:T(128)S(1)} %get-tuple-element.26.cols_ref.refs_1_, s32[24]{0:T(128)S(1)} %fusion.9.live_ref.refs_2_, s32[2]{0:T(128)S(1)} %pad_add_fusion.place_ref.refs_6_, f32[2,32768]{1,0:T(2,128)S(1)} %copy-done, ...), custom_call_target="tpu_custom_call" | custom-call | flops 37748736000 | bytes 25165824 | tf_op jit(solution)/shard_map/tiles/pallas_call | solution.py:126
  46.9 0.0 copy-done.5
  46.9 0.0 collective-permute-done.refs_11_
  46.9 0.0 collective-permute-done.1.refs_12_
  46.9 0.0 collective-permute-done.2.refs_13_
  46.9 0.0 copy-done.1
  47.0 0.0 copy-done.4
  47.0 17.8 %adjoint.1 = (f32[16,128,512]{2,1,0:T(8,128)}, bf16[16,128,512]{2,1,0:T(8,128)(2,1)}) custom-call(s32[24]{0:T(128)S(1)} %get-tuple-element.27.rows_ref.refs_0_, s32[24]{0:T(128)S(1)} %get-tuple-element.26.cols_ref.refs_1_, s32[24]{0:T(128)S(1)} %fusion.9.live_ref.refs_2_, s32[32]{0:T(128)S(1)} %get-tuple-element.25.refs_3_, ...), custom_call_target="tpu_custom_call" | custom-call | flops 96636764160 | bytes 25165824 | tf_op jit(solution)/shard_map/adjoint/pallas_call | solution.py:256
  64.7 2.3 %dynamic-slice_bitcast_fusion.6 = (bf16[2,128,512]{2,1,0:T(8,128)(2,1)}, bf16[2,128,512]{2,1,0:T(8,128)(2,1)S(1)}, bf16[2,128,512]{2,1,0:T(8,128)(2,1)S(1)}, bf1...) fusion(bf16[8,2,128,512]{3,2,1,0:T(8,128)(2,1)} %bitcast.72, ...), kind=kLoop, calls=%fused_computation.17 | loop fusion | bytes 3670044 | tf_op jit(solution)/shard_map/jit(dynamic_index_in_dim)/squeeze | solution.py:290
  67.1 10.3 %collective-permute-start.10 = (bf16[2,128,512]{2,1,0:T(8,128)(2,1)S(1)}, bf16[2,128,512]{2,1,0:T(8,128)(2,1)S(1)}, u32[]{:S(2)}, u32[]{:S(2)}) collective-permute-start(bf16[2,128,512]{2,1,0:T(8,128)(2,1)S(1)} %get-tuple-element.17), channel_id=1, source_target_pairs={{0,20},{4,24},{8,28},{12,0},{16,4},{20,8},{24,12},{28,16},{1,21},{... | collective-permute-start | bytes 786440 | tf_op jit(solution)/shard_map/ppermute | solution.py:292
  77.4 0.0 collective-permute-start.11
  77.4 9.7 %collective-permute-start.12 = (bf16[2,128,512]{2,1,0:T(8,128)(2,1)S(1)}, bf16[2,128,512]{2,1,0:T(8,128)(2,1)S(1)}, u32[]{:S(2)}, u32[]{:S(2)}) collective-permute-start(bf16[2,128,512]{2,1,0:T(8,128)(2,1)S(1)} %get-tuple-element.15), channel_id=1, source_target_pairs={{0,28},{4,0},{8,4},{12,8},{16,12},{20,16},{24,20},{28,24},{1,29},{... | collective-permute-start | bytes 786440 | tf_op jit(solution)/shard_map/ppermute | solution.py:292
  87.1 0.2 collective-permute-start.6
  87.3 1.5 collective-permute-start.7
  88.7 0.0 collective-permute-done.10
  88.8 1.2 collective-permute-start.8
  89.9 2.8 %collective-permute-done.11 = bf16[2,128,512]{2,1,0:T(8,128)(2,1)S(1)} collective-permute-done((bf16[2,128,512]{2,1,0:T(8,128)(2,1)S(1)}, bf16[2,128,512]{2,1,0:T(8,128)(2,1)S(1)}, u32[]{:S(2)}, u32[]{:S(2)}) %collective-permute-start.11) | collective-permute-done | bytes 262176 | tf_op jit(solution)/shard_map/ppermute | solution.py:292
  92.8 14.3 %collective-permute-start.9 = (bf16[2,128,512]{2,1,0:T(8,128)(2,1)S(1)}, bf16[2,128,512]{2,1,0:T(8,128)(2,1)S(1)}, u32[]{:S(2)}, u32[]{:S(2)}) collective-permute-start(bf16[2,128,512]{2,1,0:T(8,128)(2,1)S(1)} %get-tuple-element.18), channel_id=1, source_target_pairs={{0,16},{4,20},{8,24},{12,28},{16,0},{20,4},{24,8},{28,12},{1,17},{... | collective-permute-start | bytes 786440 | tf_op jit(solution)/shard_map/ppermute | solution.py:292
  107.1 21.6 %forward.1 = (f32[8,512,128]{2,1,0:T(8,128)}, bf16[8,512,128]{2,1,0:T(8,128)(2,1)S(1)}) custom-call(s32[24]{0:T(128)S(1)} %get-tuple-element.27.rows_ref.refs_0_, s32[24]{0:T(128)S(1)} %get-tuple-element.26.cols_ref.refs_1_, s32[24]{0:T(128)S(1)} %fusion.9.live_ref.refs_2_, s32[32]{0:T(128)S(1)} %get-tuple-element.25.refs_3_, ...), custom_call_target="tpu_custom_call" | custom-call | flops 96636764160 | bytes 25165824 | tf_op jit(solution)/shard_map/forward/pallas_call | solution.py:256
  128.6 0.1 dynamic-slice_bitcast_fusion.9
  128.7 0.0 collective-permute-done.12
  128.7 0.1 collective-permute-start.3
  128.8 0.0 collective-permute-done.6
  128.8 5.8 %collective-permute-start.4 = (bf16[1024,128]{1,0:T(8,128)(2,1)S(1)}, bf16[1024,128]{1,0:T(8,128)(2,1)}, u32[]{:S(2)}, u32[]{:S(2)}) collective-permute-start(bf16[1024,128]{1,0:T(8,128)(2,1)S(1)} %get-tuple-element.23), channel_id=1, source_target_pairs={{0,2},{1,3},{2,0},{3,1},{4,6},{5,7},{6,4},{7,5},{8,10},{9,11},{10,... | collective-permute-start | bytes 786440 | tf_op jit(solution)/shard_map/ppermute | solution.py:292
  134.5 0.0 collective-permute-done.7
  134.5 0.0 collective-permute-start.5
  134.6 0.0 collective-permute-done.8
  134.6 0.0 collective-permute-done.9
  134.6 1.3 fusion.6
  135.9 1.0 copy.14
  136.9 0.0 collective-permute-done.3
  136.9 9.3 %collective-permute-done.4 = bf16[1024,128]{1,0:T(8,128)(2,1)} collective-permute-done((bf16[1024,128]{1,0:T(8,128)(2,1)S(1)}, bf16[1024,128]{1,0:T(8,128)(2,1)}, u32[]{:S(2)}, u32[]{:S(2)}) %collective-permute-start.4) | collective-permute-done | bytes 262176 | tf_op jit(solution)/shard_map/ppermute | solution.py:292
  146.2 0.6 collective-permute-done.5
  146.8 2.1 %fusion.8 = f32[1024,128]{1,0:T(8,128)} fusion(bf16[1024,128]{1,0:T(8,128)(2,1)} %collective-permute-done.5, bf16[1024,128]{1,0:T(8,128)(2,1)} %collective-permute-done.4, bf16[1024,128]{1,0:T(8,128)(2,1)S(1)} %collective-permute-done.3, f32[4,1024,128]{2,1,0:T(8,128)} %bitcast.74, s32[]{:T(128)S(6)} %select_n.40), kind=kLoop, calls=%fused_computation.10 | loop fusion | flops 786432 | bytes 1835012 | tf_op jit(solution)/shard_map/add | solution.py:295
  (7 shorter events, 0.0 us)
Async XLA Ops:
  7.2 99.9 %all-gather.2.cloned.1.call-start = ((), (), s32[]{:S(2)}) async-start(), calls=%async_computation | async-start | bytes 2359296 | tf_op jit(solution)/shard_map/all_gather | solution.py:317
  7.2 39.7 %collective-permute-start = (bf16[1024,128]{1,0:T(8,128)(2,1)}, bf16[1024,128]{1,0:T(8,128)(2,1)S(1)}, u32[]{:S(2)}, u32[]{:S(2)}) collective-permute-start(bf16[1024,128]{1,0:T(8,128)(2,1)} %refs_10_.1), channel_id=1, source_target_pairs={{0,1},{1,2},{2,3},{3,0},{4,5},{5,6},{6,7},{7,4},{8,9},{9,10},{10,1... | collective-permute-start | bytes 786440 | tf_op jit(solution)/shard_map/ppermute | solution.py:319
  9.9 37.1 %collective-permute-start.1 = (bf16[1024,128]{1,0:T(8,128)(2,1)}, bf16[1024,128]{1,0:T(8,128)(2,1)S(1)}, u32[]{:S(2)}, u32[]{:S(2)}) collective-permute-start(bf16[1024,128]{1,0:T(8,128)(2,1)} %refs_10_.1), channel_id=1, source_target_pairs={{0,2},{1,3},{2,0},{3,1},{4,6},{5,7},{6,4},{7,5},{8,10},{9,11},{10,... | collective-permute-start | bytes 786440 | tf_op jit(solution)/shard_map/ppermute | solution.py:319
  9.9 37.1 %collective-permute-start.2 = (bf16[1024,128]{1,0:T(8,128)(2,1)}, bf16[1024,128]{1,0:T(8,128)(2,1)S(1)}, u32[]{:S(2)}, u32[]{:S(2)}) collective-permute-start(bf16[1024,128]{1,0:T(8,128)(2,1)} %refs_10_.1), channel_id=1, source_target_pairs={{0,3},{1,0},{2,1},{3,2},{4,7},{5,4},{6,5},{7,6},{8,11},{9,8},{10,9... | collective-permute-start | bytes 786440 | tf_op jit(solution)/shard_map/ppermute | solution.py:319
  12.6 1.0 copy-start
  13.6 0.9 copy-start.2
  14.5 0.9 copy-start.3
  15.4 31.6 %copy-start.5 = (s32[1,1,2,32]{3,2,1,0:T(2,128)S(1)}, s32[1,1,2,32]{3,2,1,0:T(2,128)}, u32[]{:S(2)}) copy-start(s32[1,1,2,32]{3,2,1,0:T(2,128)} %param.20) | copy-start | bytes 772
  15.4 31.6 %copy-start.1 = (bf16[1024,128]{1,0:T(8,128)(2,1)S(1)}, bf16[1024,128]{1,0:T(8,128)(2,1)}, u32[]{:S(2)}) copy-start(bf16[1024,128]{1,0:T(8,128)(2,1)} %refs_10_.1) | copy-start | bytes 786436
  15.4 31.6 %copy-start.4 = (s32[1,1,32]{2,1,0:T(1,128)S(1)}, s32[1,1,32]{2,1,0:T(1,128)}, u32[]{:S(2)}) copy-start(s32[1,1,32]{2,1,0:T(1,128)} %param.21) | copy-start | bytes 388
  67.1 21.7 %collective-permute-start.10 = (bf16[2,128,512]{2,1,0:T(8,128)(2,1)S(1)}, bf16[2,128,512]{2,1,0:T(8,128)(2,1)S(1)}, u32[]{:S(2)}, u32[]{:S(2)}) collective-permute-start(bf16[2,128,512]{2,1,0:T(8,128)(2,1)S(1)} %get-tuple-element.17), channel_id=1, source_target_pairs={{0,20},{4,24},{8,28},{12,0},{16,4},{20,8},{24,12},{28,16},{1,21},{... | collective-permute-start | bytes 786440 | tf_op jit(solution)/shard_map/ppermute | solution.py:292
  77.4 15.4 %collective-permute-start.11 = (bf16[2,128,512]{2,1,0:T(8,128)(2,1)S(1)}, bf16[2,128,512]{2,1,0:T(8,128)(2,1)S(1)}, u32[]{:S(2)}, u32[]{:S(2)}) collective-permute-start(bf16[2,128,512]{2,1,0:T(8,128)(2,1)S(1)} %get-tuple-element.16), channel_id=1, source_target_pairs={{0,24},{4,28},{8,0},{12,4},{16,8},{20,12},{24,16},{28,20},{1,25},{... | collective-permute-start | bytes 786440 | tf_op jit(solution)/shard_map/ppermute | solution.py:292
  77.4 51.3 %collective-permute-start.12 = (bf16[2,128,512]{2,1,0:T(8,128)(2,1)S(1)}, bf16[2,128,512]{2,1,0:T(8,128)(2,1)S(1)}, u32[]{:S(2)}, u32[]{:S(2)}) collective-permute-start(bf16[2,128,512]{2,1,0:T(8,128)(2,1)S(1)} %get-tuple-element.15), channel_id=1, source_target_pairs={{0,28},{4,0},{8,4},{12,8},{16,12},{20,16},{24,20},{28,24},{1,29},{... | collective-permute-start | bytes 786440 | tf_op jit(solution)/shard_map/ppermute | solution.py:292
  87.1 41.7 %collective-permute-start.6 = (bf16[2,128,512]{2,1,0:T(8,128)(2,1)}, bf16[2,128,512]{2,1,0:T(8,128)(2,1)S(1)}, u32[]{:S(2)}, u32[]{:S(2)}) collective-permute-start(bf16[2,128,512]{2,1,0:T(8,128)(2,1)} %get-tuple-element.14), channel_id=1, source_target_pairs={{0,4},{4,8},{8,12},{12,16},{16,20},{20,24},{24,28},{28,0},{1,5},{5... | collective-permute-start | bytes 786440 | tf_op jit(solution)/shard_map/ppermute | solution.py:292
  87.3 47.3 %collective-permute-start.7 = (bf16[2,128,512]{2,1,0:T(8,128)(2,1)}, bf16[2,128,512]{2,1,0:T(8,128)(2,1)S(1)}, u32[]{:S(2)}, u32[]{:S(2)}) collective-permute-start(bf16[2,128,512]{2,1,0:T(8,128)(2,1)} %get-tuple-element.20), channel_id=1, source_target_pairs={{0,8},{4,12},{8,16},{12,20},{16,24},{20,28},{24,0},{28,4},{1,9},{5... | collective-permute-start | bytes 786440 | tf_op jit(solution)/shard_map/ppermute | solution.py:292
  88.8 45.8 %collective-permute-start.8 = (bf16[2,128,512]{2,1,0:T(8,128)(2,1)}, bf16[2,128,512]{2,1,0:T(8,128)(2,1)S(1)}, u32[]{:S(2)}, u32[]{:S(2)}) collective-permute-start(bf16[2,128,512]{2,1,0:T(8,128)(2,1)} %get-tuple-element.19), channel_id=1, source_target_pairs={{0,12},{4,16},{8,20},{12,24},{16,28},{20,0},{24,4},{28,8},{1,13},{... | collective-permute-start | bytes 786440 | tf_op jit(solution)/shard_map/ppermute | solution.py:292
  92.8 41.8 %collective-permute-start.9 = (bf16[2,128,512]{2,1,0:T(8,128)(2,1)S(1)}, bf16[2,128,512]{2,1,0:T(8,128)(2,1)S(1)}, u32[]{:S(2)}, u32[]{:S(2)}) collective-permute-start(bf16[2,128,512]{2,1,0:T(8,128)(2,1)S(1)} %get-tuple-element.18), channel_id=1, source_target_pairs={{0,16},{4,20},{8,24},{12,28},{16,0},{20,4},{24,8},{28,12},{1,17},{... | collective-permute-start | bytes 786440 | tf_op jit(solution)/shard_map/ppermute | solution.py:292
  128.7 8.2 %collective-permute-start.3 = (bf16[1024,128]{1,0:T(8,128)(2,1)S(1)}, bf16[1024,128]{1,0:T(8,128)(2,1)S(1)}, u32[]{:S(2)}, u32[]{:S(2)}) collective-permute-start(bf16[1024,128]{1,0:T(8,128)(2,1)S(1)} %get-tuple-element.21), channel_id=1, source_target_pairs={{0,1},{1,2},{2,3},{3,0},{4,5},{5,6},{6,7},{7,4},{8,9},{9,10},{10,1... | collective-permute-start | bytes 786440 | tf_op jit(solution)/shard_map/ppermute | solution.py:292
  128.8 17.4 %collective-permute-start.4 = (bf16[1024,128]{1,0:T(8,128)(2,1)S(1)}, bf16[1024,128]{1,0:T(8,128)(2,1)}, u32[]{:S(2)}, u32[]{:S(2)}) collective-permute-start(bf16[1024,128]{1,0:T(8,128)(2,1)S(1)} %get-tuple-element.23), channel_id=1, source_target_pairs={{0,2},{1,3},{2,0},{3,1},{4,6},{5,7},{6,4},{7,5},{8,10},{9,11},{10,... | collective-permute-start | bytes 786440 | tf_op jit(solution)/shard_map/ppermute | solution.py:292
  134.5 12.3 %collective-permute-start.5 = (bf16[1024,128]{1,0:T(8,128)(2,1)S(1)}, bf16[1024,128]{1,0:T(8,128)(2,1)}, u32[]{:S(2)}, u32[]{:S(2)}) collective-permute-start(bf16[1024,128]{1,0:T(8,128)(2,1)S(1)} %get-tuple-element.22), channel_id=1, source_target_pairs={{0,3},{1,0},{2,1},{3,2},{4,7},{5,4},{6,5},{7,6},{8,11},{9,8},{10,9... | collective-permute-start | bytes 786440 | tf_op jit(solution)/shard_map/ppermute | solution.py:292
Sparse Core Ops, SparseCore 0:
  10.5 49.8 all-gather.1
where the time goes:
time: 155 us; the launch traced here: 156 us
  Pallas kernels  70.9 us (46%)
  starting transfers between devices  46.1 us (30%)
  between operations  14.1 us (9%)
  waiting for transfers between devices  12.8 us (8%)
  local copies, waits for them, and re-layouts  6.99 us (5%)
  other arithmetic  4.84 us (3%)
    ppermute x10, starting transfers between devices, scatter_sum(): lax.ppermute(piece, axis, [(at, (at + shift) % size) for at in range(size)])  43 us
    pallas_call x2, Pallas kernels, apply_blocks(): pl.pallas_call(body, out_shape=(jax.ShapeDtypeStruct(out_shape, jnp.float...  39.3 us
    pallas_call x1, Pallas kernels, make_tiles(): pl.pallas_call(tile_kernel, out_shape=jax.ShapeDtypeStruct((count, 2, LEA...  31.5 us
    ppermute x10, waiting for transfers between devices, scatter_sum(): lax.ppermute(piece, axis, [(at, (at + shift) % size) for at in range(size)])  12.8 us
    ppermute x3, starting transfers between devices, per_device(): lax.ppermute(adjoint_sources, 'col', [(at, (at + shift) % col_size) for a...  3.13 us
  transfers between devices with their start and end apart: 14, of which 3 were waited for; matrix products, arithmetic and copies ran while one was open for 4% of the time, Pallas kernels for 45%

commit v1 on v0

--- a/solution.py
+++ b/solution.py
@@ -1,3 +1,4 @@
+import functools
 import math
 
 import jax
@@ -43,8 +44,8 @@
     return jnp.concatenate([-panel[..., half:, :], panel[..., :half, :]], axis=-2)
 
 
-def params():
-    return pltpu.CompilerParams(vmem_limit_bytes=52 * 1024 * 1024)
+def params(mebibytes):
+    return pltpu.CompilerParams(vmem_limit_bytes=mebibytes * 1024 * 1024)
 
 
 def tile_kernel(
@@ -142,7 +143,7 @@
                 pltpu.VMEM((col_count, 8, LEAF), jnp.float32),
             ],
         ),
-        compiler_params=params(),
+        compiler_params=params(60),
         cost_estimate=pl.CostEstimate(
             flops=60 * count * LEAF * LEAF * 100, bytes_accessed=count * 4 * LEAF * LEAF, transcendentals=0
         ),
@@ -165,10 +166,22 @@
     return both.astype(jnp.bfloat16)
 
 
+def hand_out(total, index, own, pieces):
+    size = len(pieces) + 1
+    leaves = total.shape[0] // size
+    for local in range(leaves):
+        own[local] = total[index * leaves + local]
+    for shift, piece in enumerate(pieces, 1):
+        target = lax.rem(index + shift, size)
+        for local in range(leaves):
+            piece[local] = total[target * leaves + local].astype(jnp.bfloat16)
+
+
 def adjoint_kernel(
-    per_step, nr, nc, live, fr, fc, rank, place, tiles, left, right, *rest
+    size, per_step, nr, nc, live, fr, fc, rank, place, tiles, left, right, *rest
 ):
-    *pieces, total, narrow, panel, turned = rest
+    *rest, total, panel, turned = rest
+    pieces, own, sent = rest[:size], rest[size], rest[size + 1 :]
     step = pl.program_id(0)
     near_per, far_per = per_step
 
@@ -198,12 +211,13 @@
 
     @pl.when(step == pl.num_programs(0) - 1)
     def _():
-        narrow[...] = total[...].astype(jnp.bfloat16)
+        hand_out(total, place[0], own, sent)
 
 
 def forward_kernel(
-    per_step, nr, nc, live, fr, fc, rank, place, tiles, left, right, source, total, narrow, flat, turned
+    per_step, nr, nc, live, fr, fc, rank, place, tiles, left, right, source, own, *rest
 ):
+    *sent, total, flat, turned = rest
     step = pl.program_id(0)
     near_per, far_per = per_step
 
@@ -235,13 +249,14 @@
 
     @pl.when(step == pl.num_programs(0) - 1)
     def _():
-        narrow[...] = total[...].astype(jnp.bfloat16)
-
-
-def apply_blocks(kernel, name, lists, tiles, panels, left, right, out_shape, scratch):
+        hand_out(total, place[1], own, sent)
+
+
+def apply_blocks(kernel, name, lists, tiles, panels, left, right, out_shape, size, scratch):
     near_count = tiles.shape[0]
     far_count = left.shape[0]
     steps = math.gcd(near_count, far_count)
+    piece_shape = (out_shape[0] // size,) + out_shape[1:]
     near_per, far_per = near_count // steps, far_count // steps
 
     def whole(shape):
@@ -255,10 +270,8 @@
 
     return pl.pallas_call(
         body,
-        out_shape=(
-            jax.ShapeDtypeStruct(out_shape, jnp.float32),
-            jax.ShapeDtypeStruct(out_shape, jnp.bfloat16),
-        ),
+        out_shape=[jax.ShapeDtypeStruct(piece_shape, jnp.float32)]
+        + [jax.ShapeDtypeStruct(piece_shape, jnp.bfloat16)] * (size - 1),
         grid_spec=pltpu.PrefetchScalarGridSpec(
             num_scalar_prefetch=7,
             grid=(steps,),
@@ -268,10 +281,11 @@
                 factor,
                 *[whole(panel.shape) for panel in panels],
             ],
-            out_specs=(whole(out_shape), whole(out_shape)),
-            scratch_shapes=[pltpu.VMEM(shape, jnp.bfloat16) for shape in scratch],
+            out_specs=[whole(piece_shape)] * size,
+            scratch_shapes=[pltpu.VMEM(out_shape, jnp.float32)]
+            + [pltpu.VMEM(shape, jnp.bfloat16) for shape in scratch],
         ),
-        compiler_params=params(),
+        compiler_params=params(60),
         cost_estimate=pl.CostEstimate(
             flops=near_count * 4 * LEAF * LEAF * LANES * 30, bytes_accessed=near_count * 4 * LEAF * LEAF, transcendentals=0
         ),
@@ -279,18 +293,13 @@
     )(*lists, tiles, left, right, *panels)
 
 
-def scatter_sum(wide, narrow, axis, index, size):
-    unit = (wide.shape[0] * wide.shape[1]) // size
-    wide = wide.reshape((size, unit) + wide.shape[2:])
-    narrow = narrow.reshape((size, unit) + narrow.shape[2:])
-    own = lax.dynamic_index_in_dim(wide, index, 0, keepdims=False)
-    arrived = []
-    for shift in range(1, size):
-        target = lax.rem(index + shift, size)
-        piece = lax.dynamic_index_in_dim(narrow, target, 0, keepdims=False)
-        arrived.append(
-            lax.ppermute(piece, axis, [(at, (at + shift) % size) for at in range(size)])
-        )
+def scatter_sum(pieces, axis):
+    size = len(pieces)
+    own = pieces[0]
+    arrived = [
+        lax.ppermute(piece, axis, [(at, (at + shift) % size) for at in range(size)])
+        for shift, piece in enumerate(pieces[1:], 1)
+    ]
     for piece in arrived:
         own = own + piece.astype(jnp.float32)
     return own
@@ -332,8 +341,6 @@
         left = far_left[0, 0]
         right = far_right[0, 0]
 
-        row_span = row_count * LEAF
-        col_span = col_count * LEAF
         place = jnp.stack([row_index, col_index]).astype(jnp.int32)
         tiles = make_tiles(
             near_rows,
@@ -349,8 +356,8 @@
         )
 
         lists = (near_rows, near_cols, live, far_rows, far_cols, ranks, place)
-        adjoint_wide, adjoint_narrow = apply_blocks(
-            adjoint_kernel,
+        adjoint_parts = apply_blocks(
+            functools.partial(adjoint_kernel, col_size),
             "adjoint",
             lists,
             tiles,
@@ -358,11 +365,12 @@
             left,
             right,
             (col_count, width, LEAF),
+            row_size,
             [(row_count, width, LEAF)] * 2,
         )
-        adjoint_narrow, tiles = lax.optimization_barrier((adjoint_narrow, tiles))
-
-        field_wide, field_narrow = apply_blocks(
+        adjoint_parts, tiles = lax.optimization_barrier((adjoint_parts, tiles))
+
+        field_parts = apply_blocks(
             forward_kernel,
             "forward",
             lists,
@@ -371,37 +379,16 @@
             left,
             right,
             (row_count, LEAF, width),
+            col_size,
             [(col_count, width, LEAF), (col_count, LEAF, width)],
         )
 
-        unit = col_span // row_size
-        if unit % LEAF == 0:
-            adjoint = scatter_sum(
-                adjoint_wide.reshape(row_size, -1, width, LEAF),
-                adjoint_narrow.reshape(row_size, -1, width, LEAF),
-                "row",
-                row_index,
-                row_size,
-            )
-            adjoint_field = adjoint.transpose(0, 2, 1).reshape(unit, width)
-        else:
-            adjoint = scatter_sum(
-                adjoint_wide.transpose(0, 2, 1).reshape(row_size, unit, width),
-                adjoint_narrow.transpose(0, 2, 1).reshape(row_size, unit, width),
-                "row",
-                row_index,
-                row_size,
-            )
-            adjoint_field = adjoint.reshape(unit, width)
-        unit = row_span // col_size
-        field = scatter_sum(
-            field_wide.reshape(col_size, unit, width),
-            field_narrow.reshape(col_size, unit, width),
-            "col",
-            col_index,
-            col_size,
-        )
-        return (field.reshape(unit, width), adjoint_field)
+        late = (adjoint_parts[1], adjoint_parts[-1])
+        late, field_parts = lax.optimization_barrier((late, field_parts))
+        adjoint_parts = [adjoint_parts[0], late[0], *adjoint_parts[2:-1], late[1]]
+        adjoint = scatter_sum(adjoint_parts, "row")
+        field = scatter_sum(field_parts, "col")
+        return (field.reshape(-1, width), adjoint.transpose(0, 2, 1).reshape(-1, width))
 
     return per_device
 

time: 155 us -> 147 us (0.948)
  the two profiles are of different devices: /device:TPU:1 before, /device:TPU:29 now
where the time goes in v1:
time: 147 us; the launch traced here: 145 us
  Pallas kernels  76.2 us (52%)
  starting transfers between devices  31 us (21%)
  waiting for transfers between devices  15.8 us (11%)
  between operations  14.1 us (10%)
  local copies, waits for them, and re-layouts  4.55 us (3%)
  other arithmetic  3.56 us (2%)
    pallas_call x2, Pallas kernels, apply_blocks(): pl.pallas_call(body, out_shape=[jax.ShapeDtypeStruct(piece_shape, jnp.flo...  39.1 us
    pallas_call x1, Pallas kernels, make_tiles(): pl.pallas_call(tile_kernel, out_shape=jax.ShapeDtypeStruct((count, 2, LEA...  37 us
    ppermute x10, starting transfers between devices, scatter_sum(): lax.ppermute(piece, axis, [(at, (at + shift) % size) for at in range(size)])  28.6 us
    ppermute x10, waiting for transfers between devices, scatter_sum(): lax.ppermute(piece, axis, [(at, (at + shift) % size) for at in range(size)])  15.8 us
  transfers between devices with their start and end apart: 14, of which 3 were waited for; matrix products, arithmetic and copies ran while one was open for 4% of the time, Pallas kernels for 52%

profile of v1, /device:TPU:29, one launch (start us, length us, event | category | flops | bytes accessed | tf_op | source)
XLA Modules:
  0.0 145.2 jit_solution(18079184951935696372)
XLA Ops:
  7.2 0.0 all-gather.2.cloned.1.call-start
  7.2 1.3 collective-permute-start.1
  8.5 1.1 collective-permute-start
  9.6 0.0 collective-permute-start.2
  9.6 0.0 all-gather.2.cloned.1.call-update
  9.6 1.1 fusion.live_ref.refs_2_
  10.8 0.7 broadcast_multiply_fusion
  11.4 1.4 slice_bitcast_fusion.2
  12.8 0.6 pad_add_fusion.place_ref.refs_6_
  13.4 0.8 broadcast_in_dim.14.waves
  14.1 37.0 %tiles.1.refs_7_ = bf16[24,2,512,512]{3,2,1,0:T(8,128)(2,1)} custom-call(s32[24]{0:T(128)} %get-tuple-element.59.rows_ref.refs_0_, s32[24]{0:T(128)} %get-tuple-element.58.cols_ref.refs_1_, s32[24]{0:T(128)} %fusion.live_ref.refs_2_, s32[2]{0:T(128)} %pad_add_fusion.place_ref.refs_6_, f32[2,32768]{1,0:T(2,128)} %col_points.1, f32[2,32768]{1,0:T(2,128)} %col_points.1, ...), custom_call_target="tpu_custom_call" | custom-call | flops 37748736000 | bytes 25165824 | tf_op jit(solution)/shard_map/tiles/pallas_call | solution.py:127
  51.2 0.0 copy-done.2
  51.2 0.5 slice_bitcast_fusion
  51.7 0.0 collective-permute-done.1.refs_12_
  51.7 0.0 collective-permute-done.refs_11_
  51.7 0.0 copy-start.6
  51.8 0.0 collective-permute-done.2.refs_13_
  51.8 0.0 copy-start.7
  51.8 0.7 copy-done.5
  52.4 0.1 copy-done.6
  52.5 0.1 copy-done.7
  52.6 17.5 %adjoint.1 = (f32[2,128,512]{2,1,0:T(8,128)}, bf16[2,128,512]{2,1,0:T(8,128)(2,1)}, bf16[2,128,512]{2,1,0:T(8,128)(2,1)}, bf16[2,128,512]{2,1,0:T(8,128)(2,1)}, ...) custom-call(s32[24]{0:T(128)} %get-tuple-element.59.rows_ref.refs_0_, ...), custom_call_target="tpu_custom_call" | custom-call | flops 96636764160 | bytes 25165824 | tf_op jit(solution)/shard_map/adjoint/pallas_call | solution.py:271
  70.1 11.9 %collective-permute-start.7 = (bf16[2,128,512]{2,1,0:T(8,128)(2,1)}, bf16[2,128,512]{2,1,0:T(8,128)(2,1)S(1)}, u32[]{:S(2)}, u32[]{:S(2)}) collective-permute-start(bf16[2,128,512]{2,1,0:T(8,128)(2,1)} %get-tuple-element.50), channel_id=1, source_target_pairs={{0,8},{4,12},{8,16},{12,20},{16,24},{20,28},{24,0},{28,4},{1,9},{5... | collective-permute-start | bytes 786440 | tf_op jit(solution)/shard_map/ppermute | solution.py:300
  82.1 0.0 collective-permute-start.8
  82.1 0.2 collective-permute-start.9
  82.3 2.3 %collective-permute-start.10 = (bf16[2,128,512]{2,1,0:T(8,128)(2,1)}, bf16[2,128,512]{2,1,0:T(8,128)(2,1)S(1)}, u32[]{:S(2)}, u32[]{:S(2)}) collective-permute-start(bf16[2,128,512]{2,1,0:T(8,128)(2,1)} %get-tuple-element.53), channel_id=1, source_target_pairs={{0,20},{4,24},{8,28},{12,0},{16,4},{20,8},{24,12},{28,16},{1,21},{... | collective-permute-start | bytes 786440 | tf_op jit(solution)/shard_map/ppermute | solution.py:300
  84.6 2.3 %collective-permute-start.11 = (bf16[2,128,512]{2,1,0:T(8,128)(2,1)}, bf16[2,128,512]{2,1,0:T(8,128)(2,1)S(1)}, u32[]{:S(2)}, u32[]{:S(2)}) collective-permute-start(bf16[2,128,512]{2,1,0:T(8,128)(2,1)} %get-tuple-element.54), channel_id=1, source_target_pairs={{0,24},{4,28},{8,0},{12,4},{16,8},{20,12},{24,16},{28,20},{1,25},{... | collective-permute-start | bytes 786440 | tf_op jit(solution)/shard_map/ppermute | solution.py:300
  86.9 21.6 %forward.1 = (f32[2,512,128]{2,1,0:T(8,128)}, bf16[2,512,128]{2,1,0:T(8,128)(2,1)}, bf16[2,512,128]{2,1,0:T(8,128)(2,1)}, bf16[2,512,128]{2,1,0:T(8,128)(2,1)}) custom-call(s32[24]{0:T(128)} %get-tuple-element.59.rows_ref.refs_0_, s32[24]{0:T(128)} %get-tuple-element.58.cols_ref.refs_1_, s32[24]{0:T(128)} %fusion.live_ref.refs_2_, ...), custom_call_target="tpu_custom_call" | custom-call | flops 96636764160 | bytes 25165824 | tf_op jit(solution)/shard_map/forward/pallas_call | solution.py:271
  108.5 0.0 collective-permute-done.7
  108.5 0.0 copy-done.4
  108.5 1.7 %collective-permute-start.6 = (bf16[2,128,512]{2,1,0:T(8,128)(2,1)S(1)}, bf16[2,128,512]{2,1,0:T(8,128)(2,1)S(1)}, u32[]{:S(2)}, u32[]{:S(2)}) collective-permute-start(bf16[2,128,512]{2,1,0:T(8,128)(2,1)S(1)} %copy-done.4), channel_id=1, source_target_pairs={{0,4},{4,8},{8,12},{12,16},{16,20},{20,24},{24,28},{28,0},{1,5},{5... | collective-permute-start | bytes 786440 | tf_op jit(solution)/shard_map/ppermute | solution.py:300
  110.3 0.0 collective-permute-done.8
  110.3 0.0 collective-permute-start.12
  110.3 6.4 %collective-permute-done.9 = bf16[2,128,512]{2,1,0:T(8,128)(2,1)S(1)} collective-permute-done((bf16[2,128,512]{2,1,0:T(8,128)(2,1)}, bf16[2,128,512]{2,1,0:T(8,128)(2,1)S(1)}, u32[]{:S(2)}, u32[]{:S(2)}) %collective-permute-start.9) | collective-permute-done | bytes 262176 | tf_op jit(solution)/shard_map/ppermute | solution.py:300
  116.7 3.7 %collective-permute-start.3 = (bf16[2,512,128]{2,1,0:T(8,128)(2,1)}, bf16[2,512,128]{2,1,0:T(8,128)(2,1)S(1)}, u32[]{:S(2)}, u32[]{:S(2)}) collective-permute-start(bf16[2,512,128]{2,1,0:T(8,128)(2,1)} %get-tuple-element.45), channel_id=1, source_target_pairs={{0,1},{1,2},{2,3},{3,0},{4,5},{5,6},{6,7},{7,4},{8,9},{9,10},{10,1... | collective-permute-start | bytes 786440 | tf_op jit(solution)/shard_map/ppermute | solution.py:300
  120.4 0.0 collective-permute-done.10
  120.4 4.6 %collective-permute-start.4 = (bf16[2,512,128]{2,1,0:T(8,128)(2,1)}, bf16[2,512,128]{2,1,0:T(8,128)(2,1)S(1)}, u32[]{:S(2)}, u32[]{:S(2)}) collective-permute-start(bf16[2,512,128]{2,1,0:T(8,128)(2,1)} %get-tuple-element.46), channel_id=1, source_target_pairs={{0,2},{1,3},{2,0},{3,1},{4,6},{5,7},{6,4},{7,5},{8,10},{9,11},{10,... | collective-permute-start | bytes 786440 | tf_op jit(solution)/shard_map/ppermute | solution.py:300
  125.0 0.0 collective-permute-done.11
  125.0 1.7 %collective-permute-start.5 = (bf16[2,512,128]{2,1,0:T(8,128)(2,1)}, bf16[2,512,128]{2,1,0:T(8,128)(2,1)S(1)}, u32[]{:S(2)}, u32[]{:S(2)}) collective-permute-start(bf16[2,512,128]{2,1,0:T(8,128)(2,1)} %get-tuple-element.47), channel_id=1, source_target_pairs={{0,3},{1,0},{2,1},{3,2},{4,7},{5,4},{6,5},{7,6},{8,11},{9,8},{10,9... | collective-permute-start | bytes 786440 | tf_op jit(solution)/shard_map/ppermute | solution.py:300
  126.8 0.0 collective-permute-done.6
  126.8 0.0 collective-permute-done.12
  126.8 0.3 add_bitcast_fusion
  127.1 1.0 copy.14
  128.1 0.0 collective-permute-done.3
  128.1 5.9 %collective-permute-done.4 = bf16[2,512,128]{2,1,0:T(8,128)(2,1)S(1)} collective-permute-done((bf16[2,512,128]{2,1,0:T(8,128)(2,1)}, bf16[2,512,128]{2,1,0:T(8,128)(2,1)S(1)}, u32[]{:S(2)}, u32[]{:S(2)}) %collective-permute-start.4) | collective-permute-done | bytes 262176 | tf_op jit(solution)/shard_map/ppermute | solution.py:300
  134.0 3.4 %collective-permute-done.5 = bf16[2,512,128]{2,1,0:T(8,128)(2,1)S(1)} collective-permute-done((bf16[2,512,128]{2,1,0:T(8,128)(2,1)}, bf16[2,512,128]{2,1,0:T(8,128)(2,1)S(1)}, u32[]{:S(2)}, u32[]{:S(2)}) %collective-permute-start.5) | collective-permute-done | bytes 262176 | tf_op jit(solution)/shard_map/ppermute | solution.py:300
  137.4 0.0 copy-done
  137.4 0.9 convert_add_fusion
  (9 shorter events, 0.0 us)
Async XLA Ops:
  7.2 79.8 %all-gather.2.cloned.1.call-start = ((), (), s32[]{:S(2)}) async-start(), calls=%async_computation | async-start | bytes 2359296 | tf_op jit(solution)/shard_map/all_gather | solution.py:326
  7.2 44.5 %collective-permute-start.1 = (bf16[1024,128]{1,0:T(8,128)(2,1)}, bf16[1024,128]{1,0:T(8,128)(2,1)S(1)}, u32[]{:S(2)}, u32[]{:S(2)}) collective-permute-start(bf16[1024,128]{1,0:T(8,128)(2,1)} %refs_10_.1), channel_id=1, source_target_pairs={{0,2},{1,3},{2,0},{3,1},{4,6},{5,7},{6,4},{7,5},{8,10},{9,11},{10,... | collective-permute-start | bytes 786440 | tf_op jit(solution)/shard_map/ppermute | solution.py:328
  8.5 43.3 %collective-permute-start = (bf16[1024,128]{1,0:T(8,128)(2,1)}, bf16[1024,128]{1,0:T(8,128)(2,1)S(1)}, u32[]{:S(2)}, u32[]{:S(2)}) collective-permute-start(bf16[1024,128]{1,0:T(8,128)(2,1)} %refs_10_.1), channel_id=1, source_target_pairs={{0,1},{1,2},{2,3},{3,0},{4,5},{5,6},{6,7},{7,4},{8,9},{9,10},{10,1... | collective-permute-start | bytes 786440 | tf_op jit(solution)/shard_map/ppermute | solution.py:328
  9.6 42.2 %collective-permute-start.2 = (bf16[1024,128]{1,0:T(8,128)(2,1)}, bf16[1024,128]{1,0:T(8,128)(2,1)S(1)}, u32[]{:S(2)}, u32[]{:S(2)}) collective-permute-start(bf16[1024,128]{1,0:T(8,128)(2,1)} %refs_10_.1), channel_id=1, source_target_pairs={{0,3},{1,0},{2,1},{3,2},{4,7},{5,4},{6,5},{7,6},{8,11},{9,8},{10,9... | collective-permute-start | bytes 786440 | tf_op jit(solution)/shard_map/ppermute | solution.py:328
  14.1 37.0 %copy-start.2 = (s32[1,1,2,32]{3,2,1,0:T(2,128)S(1)}, s32[1,1,2,32]{3,2,1,0:T(2,128)}, u32[]{:S(2)}) copy-start(s32[1,1,2,32]{3,2,1,0:T(2,128)} %param.20) | copy-start | bytes 772
  51.7 0.7 copy-start.5
  51.7 0.8 copy-start.6
  51.8 0.9 copy-start.7
  70.1 38.4 %collective-permute-start.7 = (bf16[2,128,512]{2,1,0:T(8,128)(2,1)}, bf16[2,128,512]{2,1,0:T(8,128)(2,1)S(1)}, u32[]{:S(2)}, u32[]{:S(2)}) collective-permute-start(bf16[2,128,512]{2,1,0:T(8,128)(2,1)} %get-tuple-element.50), channel_id=1, source_target_pairs={{0,8},{4,12},{8,16},{12,20},{16,24},{20,28},{24,0},{28,4},{1,9},{5... | collective-permute-start | bytes 786440 | tf_op jit(solution)/shard_map/ppermute | solution.py:300
  82.1 28.2 %collective-permute-start.8 = (bf16[2,128,512]{2,1,0:T(8,128)(2,1)}, bf16[2,128,512]{2,1,0:T(8,128)(2,1)S(1)}, u32[]{:S(2)}, u32[]{:S(2)}) collective-permute-start(bf16[2,128,512]{2,1,0:T(8,128)(2,1)} %get-tuple-element.51), channel_id=1, source_target_pairs={{0,12},{4,16},{8,20},{12,24},{16,28},{20,0},{24,4},{28,8},{1,13},{... | collective-permute-start | bytes 786440 | tf_op jit(solution)/shard_map/ppermute | solution.py:300
  82.1 34.6 %collective-permute-start.9 = (bf16[2,128,512]{2,1,0:T(8,128)(2,1)}, bf16[2,128,512]{2,1,0:T(8,128)(2,1)S(1)}, u32[]{:S(2)}, u32[]{:S(2)}) collective-permute-start(bf16[2,128,512]{2,1,0:T(8,128)(2,1)} %get-tuple-element.52), channel_id=1, source_target_pairs={{0,16},{4,20},{8,24},{12,28},{16,0},{20,4},{24,8},{28,12},{1,17},{... | collective-permute-start | bytes 786440 | tf_op jit(solution)/shard_map/ppermute | solution.py:300
  82.3 38.1 %collective-permute-start.10 = (bf16[2,128,512]{2,1,0:T(8,128)(2,1)}, bf16[2,128,512]{2,1,0:T(8,128)(2,1)S(1)}, u32[]{:S(2)}, u32[]{:S(2)}) collective-permute-start(bf16[2,128,512]{2,1,0:T(8,128)(2,1)} %get-tuple-element.53), channel_id=1, source_target_pairs={{0,20},{4,24},{8,28},{12,0},{16,4},{20,8},{24,12},{28,16},{1,21},{... | collective-permute-start | bytes 786440 | tf_op jit(solution)/shard_map/ppermute | solution.py:300
  84.6 40.4 %collective-permute-start.11 = (bf16[2,128,512]{2,1,0:T(8,128)(2,1)}, bf16[2,128,512]{2,1,0:T(8,128)(2,1)S(1)}, u32[]{:S(2)}, u32[]{:S(2)}) collective-permute-start(bf16[2,128,512]{2,1,0:T(8,128)(2,1)} %get-tuple-element.54), channel_id=1, source_target_pairs={{0,24},{4,28},{8,0},{12,4},{16,8},{20,12},{24,16},{28,20},{1,25},{... | collective-permute-start | bytes 786440 | tf_op jit(solution)/shard_map/ppermute | solution.py:300
  86.9 21.6 %copy-start.4 = (bf16[2,128,512]{2,1,0:T(8,128)(2,1)S(1)}, bf16[2,128,512]{2,1,0:T(8,128)(2,1)}, u32[]{:S(2)}) copy-start(bf16[2,128,512]{2,1,0:T(8,128)(2,1)} %get-tuple-element.49) | copy-start | bytes 786436
  86.9 23.4 %copy-start.3 = (bf16[2,128,512]{2,1,0:T(8,128)(2,1)S(1)}, bf16[2,128,512]{2,1,0:T(8,128)(2,1)}, u32[]{:S(2)}) copy-start(bf16[2,128,512]{2,1,0:T(8,128)(2,1)} %get-tuple-element.55) | copy-start | bytes 786436
  86.9 39.9 %copy-start.1 = (f32[2,128,512]{2,1,0:T(8,128)S(1)}, f32[2,128,512]{2,1,0:T(8,128)}, u32[]{:S(2)}) copy-start(f32[2,128,512]{2,1,0:T(8,128)} %get-tuple-element.48) | copy-start | bytes 1572868
  108.5 28.9 %copy-start = (f32[2,512,128]{2,1,0:T(8,128)S(1)}, f32[2,512,128]{2,1,0:T(8,128)}, u32[]{:S(2)}) copy-start(f32[2,512,128]{2,1,0:T(8,128)} %get-tuple-element.44) | copy-start | bytes 1572868
  108.5 18.2 %collective-permute-start.6 = (bf16[2,128,512]{2,1,0:T(8,128)(2,1)S(1)}, bf16[2,128,512]{2,1,0:T(8,128)(2,1)S(1)}, u32[]{:S(2)}, u32[]{:S(2)}) collective-permute-start(bf16[2,128,512]{2,1,0:T(8,128)(2,1)S(1)} %copy-done.4), channel_id=1, source_target_pairs={{0,4},{4,8},{8,12},{12,16},{16,20},{20,24},{24,28},{28,0},{1,5},{5... | collective-permute-start | bytes 786440 | tf_op jit(solution)/shard_map/ppermute | solution.py:300
  110.3 16.5 %collective-permute-start.12 = (bf16[2,128,512]{2,1,0:T(8,128)(2,1)S(1)}, bf16[2,128,512]{2,1,0:T(8,128)(2,1)S(1)}, u32[]{:S(2)}, u32[]{:S(2)}) collective-permute-start(bf16[2,128,512]{2,1,0:T(8,128)(2,1)S(1)} %copy-done.3), channel_id=1, source_target_pairs={{0,28},{4,0},{8,4},{12,8},{16,12},{20,16},{24,20},{28,24},{1,29},{... | collective-permute-start | bytes 786440 | tf_op jit(solution)/shard_map/ppermute | solution.py:300
  116.7 11.4 %collective-permute-start.3 = (bf16[2,512,128]{2,1,0:T(8,128)(2,1)}, bf16[2,512,128]{2,1,0:T(8,128)(2,1)S(1)}, u32[]{:S(2)}, u32[]{:S(2)}) collective-permute-start(bf16[2,512,128]{2,1,0:T(8,128)(2,1)} %get-tuple-element.45), channel_id=1, source_target_pairs={{0,1},{1,2},{2,3},{3,0},{4,5},{5,6},{6,7},{7,4},{8,9},{9,10},{10,1... | collective-permute-start | bytes 786440 | tf_op jit(solution)/shard_map/ppermute | solution.py:300
  120.4 13.6 %collective-permute-start.4 = (bf16[2,512,128]{2,1,0:T(8,128)(2,1)}, bf16[2,512,128]{2,1,0:T(8,128)(2,1)S(1)}, u32[]{:S(2)}, u32[]{:S(2)}) collective-permute-start(bf16[2,512,128]{2,1,0:T(8,128)(2,1)} %get-tuple-element.46), channel_id=1, source_target_pairs={{0,2},{1,3},{2,0},{3,1},{4,6},{5,7},{6,4},{7,5},{8,10},{9,11},{10,... | collective-permute-start | bytes 786440 | tf_op jit(solution)/shard_map/ppermute | solution.py:300
  125.0 12.4 %collective-permute-start.5 = (bf16[2,512,128]{2,1,0:T(8,128)(2,1)}, bf16[2,512,128]{2,1,0:T(8,128)(2,1)S(1)}, u32[]{:S(2)}, u32[]{:S(2)}) collective-permute-start(bf16[2,512,128]{2,1,0:T(8,128)(2,1)} %get-tuple-element.47), channel_id=1, source_target_pairs={{0,3},{1,0},{2,1},{3,2},{4,7},{5,4},{6,5},{7,6},{8,11},{9,8},{10,9... | collective-permute-start | bytes 786440 | tf_op jit(solution)/shard_map/ppermute | solution.py:300
Sparse Core Ops, SparseCore 0:
  10.1 47.6 all-gather.1

commit v2 on v1

--- a/solution.py
+++ b/solution.py
@@ -11,7 +11,7 @@
 LEAF = 512
 RMAX = 64
 LANES = 128
-CHUNK = 64
+CHUNK = 256
 
 DAMPING = 0.02
 SOFTENING = 0.01
@@ -252,10 +252,10 @@
         hand_out(total, place[1], own, sent)
 
 
-def apply_blocks(kernel, name, lists, tiles, panels, left, right, out_shape, size, scratch):
+def apply_blocks(kernel, name, merge, lists, tiles, panels, left, right, out_shape, size, scratch):
     near_count = tiles.shape[0]
     far_count = left.shape[0]
-    steps = math.gcd(near_count, far_count)
+    steps = max(1, math.gcd(near_count, far_count) // merge)
     piece_shape = (out_shape[0] // size,) + out_shape[1:]
     near_per, far_per = near_count // steps, far_count // steps
 
@@ -359,6 +359,7 @@
         adjoint_parts = apply_blocks(
             functools.partial(adjoint_kernel, col_size),
             "adjoint",
+            2,
             lists,
             tiles,
             adjoint_pieces,
@@ -373,6 +374,7 @@
         field_parts = apply_blocks(
             forward_kernel,
             "forward",
+            1,
             lists,
             tiles,
             (source_block.reshape(col_count, LEAF, width),),

time: 147 us -> 139 us (0.946)
  Pallas kernels: 76.2 us -> 62.6 us
  waiting for transfers between devices: 15.8 us -> 20.6 us
    pallas_call x1, Pallas kernels: 37 us -> 24.9 us  [make_tiles(): pl.pallas_call(tile_kernel, out_shape=jax.ShapeDtypeStruct((count, 2, LEA...]
    ppermute x10, waiting for transfers between devices: 15.8 us -> 20.6 us  [scatter_sum(): lax.ppermute(piece, axis, [(at, (at + shift) % size) for at in range(size)])]
  transfers between devices with their start and end apart: 14 -> 14, of which waited for: 3 -> 4; matrix products, arithmetic and copies ran while one was open for 4% -> 5% of each run, Pallas kernels for 52% -> 46%
where the time goes in v2:
time: 139 us; the launch traced here: 137 us
  Pallas kernels  62.6 us (45%)
  starting transfers between devices  31.6 us (23%)
  waiting for transfers between devices  20.6 us (15%)
  between operations  14.1 us (10%)
  local copies, waits for them, and re-layouts  4.56 us (3%)
  other arithmetic  3.56 us (3%)
    pallas_call x2, Pallas kernels, apply_blocks(): pl.pallas_call(body, out_shape=[jax.ShapeDtypeStruct(piece_shape, jnp.flo...  37.7 us
    ppermute x10, starting transfers between devices, scatter_sum(): lax.ppermute(piece, axis, [(at, (at + shift) % size) for at in range(size)])  29.2 us
    pallas_call x1, Pallas kernels, make_tiles(): pl.pallas_call(tile_kernel, out_shape=jax.ShapeDtypeStruct((count, 2, LEA...  24.9 us
    ppermute x10, waiting for transfers between devices, scatter_sum(): lax.ppermute(piece, axis, [(at, (at + shift) % size) for at in range(size)])  20.6 us
  transfers between devices with their start and end apart: 14, of which 4 were waited for; matrix products, arithmetic and copies ran while one was open for 5% of the time, Pallas kernels for 46%

profile of v2, /device:TPU:29, one launch (start us, length us, event | category | flops | bytes accessed | tf_op | source)
XLA Modules:
  0.0 137.1 jit_solution(17998074201689593113)
XLA Ops:
  7.2 0.0 all-gather.2.cloned.1.call-start
  7.2 1.3 collective-permute-start.1
  8.5 1.1 collective-permute-start
  9.6 0.0 collective-permute-start.2
  9.6 0.0 all-gather.2.cloned.1.call-update
  9.6 1.1 fusion.live_ref.refs_2_
  10.8 0.7 broadcast_multiply_fusion
  11.4 1.4 slice_bitcast_fusion.2
  12.8 0.6 pad_add_fusion.place_ref.refs_6_
  13.4 0.8 broadcast_in_dim.14.waves
  14.1 24.9 %tiles.1.refs_7_ = bf16[24,2,512,512]{3,2,1,0:T(8,128)(2,1)} custom-call(s32[24]{0:T(128)} %get-tuple-element.59.rows_ref.refs_0_, s32[24]{0:T(128)} %get-tuple-element.58.cols_ref.refs_1_, s32[24]{0:T(128)} %fusion.live_ref.refs_2_, s32[2]{0:T(128)} %pad_add_fusion.place_ref.refs_6_, f32[2,32768]{1,0:T(2,128)} %col_points.1, f32[2,32768]{1,0:T(2,128)} %col_points.1, ...), custom_call_target="tpu_custom_call" | custom-call | flops 37748736000 | bytes 25165824 | tf_op jit(solution)/shard_map/tiles/pallas_call | solution.py:127
  39.1 0.0 copy-done.2
  39.1 0.5 slice_bitcast_fusion
  39.6 0.0 collective-permute-done.1.refs_12_
  39.6 0.0 collective-permute-done.refs_11_
  39.6 0.0 copy-start.6
  39.6 0.0 collective-permute-done.2.refs_13_
  39.7 0.7 copy-done.5
  40.3 0.1 copy-done.6
  40.4 0.1 copy-done.7
  40.5 16.1 %adjoint.1 = (f32[2,128,512]{2,1,0:T(8,128)}, bf16[2,128,512]{2,1,0:T(8,128)(2,1)}, bf16[2,128,512]{2,1,0:T(8,128)(2,1)}, bf16[2,128,512]{2,1,0:T(8,128)(2,1)}, ...) custom-call(s32[24]{0:T(128)} %get-tuple-element.59.rows_ref.refs_0_, ...), custom_call_target="tpu_custom_call" | custom-call | flops 96636764160 | bytes 25165824 | tf_op jit(solution)/shard_map/adjoint/pallas_call | solution.py:271
  56.6 4.4 %collective-permute-start.7 = (bf16[2,128,512]{2,1,0:T(8,128)(2,1)}, bf16[2,128,512]{2,1,0:T(8,128)(2,1)S(1)}, u32[]{:S(2)}, u32[]{:S(2)}) collective-permute-start(bf16[2,128,512]{2,1,0:T(8,128)(2,1)} %get-tuple-element.50), channel_id=1, source_target_pairs={{0,8},{4,12},{8,16},{12,20},{16,24},{20,28},{24,0},{28,4},{1,9},{5... | collective-permute-start | bytes 786440 | tf_op jit(solution)/shard_map/ppermute | solution.py:300
  61.0 13.6 %collective-permute-start.8 = (bf16[2,128,512]{2,1,0:T(8,128)(2,1)}, bf16[2,128,512]{2,1,0:T(8,128)(2,1)S(1)}, u32[]{:S(2)}, u32[]{:S(2)}) collective-permute-start(bf16[2,128,512]{2,1,0:T(8,128)(2,1)} %get-tuple-element.51), channel_id=1, source_target_pairs={{0,12},{4,16},{8,20},{12,24},{16,28},{20,0},{24,4},{28,8},{1,13},{... | collective-permute-start | bytes 786440 | tf_op jit(solution)/shard_map/ppermute | solution.py:300
  74.6 0.0 collective-permute-start.9
  74.6 1.4 %collective-permute-start.10 = (bf16[2,128,512]{2,1,0:T(8,128)(2,1)}, bf16[2,128,512]{2,1,0:T(8,128)(2,1)S(1)}, u32[]{:S(2)}, u32[]{:S(2)}) collective-permute-start(bf16[2,128,512]{2,1,0:T(8,128)(2,1)} %get-tuple-element.53), channel_id=1, source_target_pairs={{0,20},{4,24},{8,28},{12,0},{16,4},{20,8},{24,12},{28,16},{1,21},{... | collective-permute-start | bytes 786440 | tf_op jit(solution)/shard_map/ppermute | solution.py:300
  76.0 0.0 collective-permute-start.11
  76.0 0.0 copy-start.1
  76.0 21.6 %forward.1 = (f32[2,512,128]{2,1,0:T(8,128)}, bf16[2,512,128]{2,1,0:T(8,128)(2,1)}, bf16[2,512,128]{2,1,0:T(8,128)(2,1)}, bf16[2,512,128]{2,1,0:T(8,128)(2,1)}) custom-call(s32[24]{0:T(128)} %get-tuple-element.59.rows_ref.refs_0_, s32[24]{0:T(128)} %get-tuple-element.58.cols_ref.refs_1_, s32[24]{0:T(128)} %fusion.live_ref.refs_2_, ...), custom_call_target="tpu_custom_call" | custom-call | flops 96636764160 | bytes 25165824 | tf_op jit(solution)/shard_map/forward/pallas_call | solution.py:271
  97.6 0.0 collective-permute-done.7
  97.7 5.2 %collective-permute-start.6 = (bf16[2,128,512]{2,1,0:T(8,128)(2,1)S(1)}, bf16[2,128,512]{2,1,0:T(8,128)(2,1)S(1)}, u32[]{:S(2)}, u32[]{:S(2)}) collective-permute-start(bf16[2,128,512]{2,1,0:T(8,128)(2,1)S(1)} %copy-done.4), channel_id=1, source_target_pairs={{0,4},{4,8},{8,12},{12,16},{16,20},{20,24},{24,28},{28,0},{1,5},{5... | collective-permute-start | bytes 786440 | tf_op jit(solution)/shard_map/ppermute | solution.py:300
  102.8 0.0 collective-permute-done.8
  102.8 0.0 copy-done.3
  102.8 2.1 %collective-permute-start.12 = (bf16[2,128,512]{2,1,0:T(8,128)(2,1)S(1)}, bf16[2,128,512]{2,1,0:T(8,128)(2,1)S(1)}, u32[]{:S(2)}, u32[]{:S(2)}) collective-permute-start(bf16[2,128,512]{2,1,0:T(8,128)(2,1)S(1)} %copy-done.3), channel_id=1, source_target_pairs={{0,28},{4,0},{8,4},{12,8},{16,12},{20,16},{24,20},{28,24},{1,29},{... | collective-permute-start | bytes 786440 | tf_op jit(solution)/shard_map/ppermute | solution.py:300
  105.0 4.5 %collective-permute-done.9 = bf16[2,128,512]{2,1,0:T(8,128)(2,1)S(1)} collective-permute-done((bf16[2,128,512]{2,1,0:T(8,128)(2,1)}, bf16[2,128,512]{2,1,0:T(8,128)(2,1)S(1)}, u32[]{:S(2)}, u32[]{:S(2)}) %collective-permute-start.9) | collective-permute-done | bytes 262176 | tf_op jit(solution)/shard_map/ppermute | solution.py:300
  109.4 0.0 collective-permute-start.3
  109.4 7.7 %collective-permute-done.10 = bf16[2,128,512]{2,1,0:T(8,128)(2,1)S(1)} collective-permute-done((bf16[2,128,512]{2,1,0:T(8,128)(2,1)}, bf16[2,128,512]{2,1,0:T(8,128)(2,1)S(1)}, u32[]{:S(2)}, u32[]{:S(2)}) %collective-permute-start.10) | collective-permute-done | bytes 262176 | tf_op jit(solution)/shard_map/ppermute | solution.py:300
  117.1 1.7 %collective-permute-start.4 = (bf16[2,512,128]{2,1,0:T(8,128)(2,1)}, bf16[2,512,128]{2,1,0:T(8,128)(2,1)S(1)}, u32[]{:S(2)}, u32[]{:S(2)}) collective-permute-start(bf16[2,512,128]{2,1,0:T(8,128)(2,1)} %get-tuple-element.46), channel_id=1, source_target_pairs={{0,2},{1,3},{2,0},{3,1},{4,6},{5,7},{6,4},{7,5},{8,10},{9,11},{10,... | collective-permute-start | bytes 786440 | tf_op jit(solution)/shard_map/ppermute | solution.py:300
  118.9 0.0 collective-permute-done.11
  118.9 0.8 collective-permute-start.5
  119.7 0.0 collective-permute-done.6
  119.7 0.0 collective-permute-done.12
  119.7 0.0 copy-done.1
  119.7 0.3 add_bitcast_fusion
  119.9 1.0 copy.14
  120.9 0.0 collective-permute-done.3
  120.9 5.0 %collective-permute-done.4 = bf16[2,512,128]{2,1,0:T(8,128)(2,1)S(1)} collective-permute-done((bf16[2,512,128]{2,1,0:T(8,128)(2,1)}, bf16[2,512,128]{2,1,0:T(8,128)(2,1)S(1)}, u32[]{:S(2)}, u32[]{:S(2)}) %collective-permute-start.4) | collective-permute-done | bytes 262176 | tf_op jit(solution)/shard_map/ppermute | solution.py:300
  126.0 3.4 %collective-permute-done.5 = bf16[2,512,128]{2,1,0:T(8,128)(2,1)S(1)} collective-permute-done((bf16[2,512,128]{2,1,0:T(8,128)(2,1)}, bf16[2,512,128]{2,1,0:T(8,128)(2,1)S(1)}, u32[]{:S(2)}, u32[]{:S(2)}) %collective-permute-start.5) | collective-permute-done | bytes 262176 | tf_op jit(solution)/shard_map/ppermute | solution.py:300
  129.3 0.9 convert_add_fusion
  (9 shorter events, 0.0 us)
Async XLA Ops:
  7.2 68.8 %all-gather.2.cloned.1.call-start = ((), (), s32[]{:S(2)}) async-start(), calls=%async_computation | async-start | bytes 2359296 | tf_op jit(solution)/shard_map/all_gather | solution.py:326
  7.2 32.4 %collective-permute-start.1 = (bf16[1024,128]{1,0:T(8,128)(2,1)}, bf16[1024,128]{1,0:T(8,128)(2,1)S(1)}, u32[]{:S(2)}, u32[]{:S(2)}) collective-permute-start(bf16[1024,128]{1,0:T(8,128)(2,1)} %refs_10_.1), channel_id=1, source_target_pairs={{0,2},{1,3},{2,0},{3,1},{4,6},{5,7},{6,4},{7,5},{8,10},{9,11},{10,... | collective-permute-start | bytes 786440 | tf_op jit(solution)/shard_map/ppermute | solution.py:328
  8.5 31.1 %collective-permute-start = (bf16[1024,128]{1,0:T(8,128)(2,1)}, bf16[1024,128]{1,0:T(8,128)(2,1)S(1)}, u32[]{:S(2)}, u32[]{:S(2)}) collective-permute-start(bf16[1024,128]{1,0:T(8,128)(2,1)} %refs_10_.1), channel_id=1, source_target_pairs={{0,1},{1,2},{2,3},{3,0},{4,5},{5,6},{6,7},{7,4},{8,9},{9,10},{10,1... | collective-permute-start | bytes 786440 | tf_op jit(solution)/shard_map/ppermute | solution.py:328
  9.6 30.1 %collective-permute-start.2 = (bf16[1024,128]{1,0:T(8,128)(2,1)}, bf16[1024,128]{1,0:T(8,128)(2,1)S(1)}, u32[]{:S(2)}, u32[]{:S(2)}) collective-permute-start(bf16[1024,128]{1,0:T(8,128)(2,1)} %refs_10_.1), channel_id=1, source_target_pairs={{0,3},{1,0},{2,1},{3,2},{4,7},{5,4},{6,5},{7,6},{8,11},{9,8},{10,9... | collective-permute-start | bytes 786440 | tf_op jit(solution)/shard_map/ppermute | solution.py:328
  14.1 24.9 %copy-start.2 = (s32[1,1,2,32]{3,2,1,0:T(2,128)S(1)}, s32[1,1,2,32]{3,2,1,0:T(2,128)}, u32[]{:S(2)}) copy-start(s32[1,1,2,32]{3,2,1,0:T(2,128)} %param.20) | copy-start | bytes 772
  39.6 0.7 copy-start.5
  39.6 0.8 copy-start.6
  39.7 0.9 copy-start.7
  56.6 41.0 %collective-permute-start.7 = (bf16[2,128,512]{2,1,0:T(8,128)(2,1)}, bf16[2,128,512]{2,1,0:T(8,128)(2,1)S(1)}, u32[]{:S(2)}, u32[]{:S(2)}) collective-permute-start(bf16[2,128,512]{2,1,0:T(8,128)(2,1)} %get-tuple-element.50), channel_id=1, source_target_pairs={{0,8},{4,12},{8,16},{12,20},{16,24},{20,28},{24,0},{28,4},{1,9},{5... | collective-permute-start | bytes 786440 | tf_op jit(solution)/shard_map/ppermute | solution.py:300
  61.0 41.8 %collective-permute-start.8 = (bf16[2,128,512]{2,1,0:T(8,128)(2,1)}, bf16[2,128,512]{2,1,0:T(8,128)(2,1)S(1)}, u32[]{:S(2)}, u32[]{:S(2)}) collective-permute-start(bf16[2,128,512]{2,1,0:T(8,128)(2,1)} %get-tuple-element.51), channel_id=1, source_target_pairs={{0,12},{4,16},{8,20},{12,24},{16,28},{20,0},{24,4},{28,8},{1,13},{... | collective-permute-start | bytes 786440 | tf_op jit(solution)/shard_map/ppermute | solution.py:300
  74.6 34.8 %collective-permute-start.9 = (bf16[2,128,512]{2,1,0:T(8,128)(2,1)}, bf16[2,128,512]{2,1,0:T(8,128)(2,1)S(1)}, u32[]{:S(2)}, u32[]{:S(2)}) collective-permute-start(bf16[2,128,512]{2,1,0:T(8,128)(2,1)} %get-tuple-element.52), channel_id=1, source_target_pairs={{0,16},{4,20},{8,24},{12,28},{16,0},{20,4},{24,8},{28,12},{1,17},{... | collective-permute-start | bytes 786440 | tf_op jit(solution)/shard_map/ppermute | solution.py:300
  74.6 42.6 %collective-permute-start.10 = (bf16[2,128,512]{2,1,0:T(8,128)(2,1)}, bf16[2,128,512]{2,1,0:T(8,128)(2,1)S(1)}, u32[]{:S(2)}, u32[]{:S(2)}) collective-permute-start(bf16[2,128,512]{2,1,0:T(8,128)(2,1)} %get-tuple-element.53), channel_id=1, source_target_pairs={{0,20},{4,24},{8,28},{12,0},{16,4},{20,8},{24,12},{28,16},{1,21},{... | collective-permute-start | bytes 786440 | tf_op jit(solution)/shard_map/ppermute | solution.py:300
  76.0 42.9 %collective-permute-start.11 = (bf16[2,128,512]{2,1,0:T(8,128)(2,1)}, bf16[2,128,512]{2,1,0:T(8,128)(2,1)S(1)}, u32[]{:S(2)}, u32[]{:S(2)}) collective-permute-start(bf16[2,128,512]{2,1,0:T(8,128)(2,1)} %get-tuple-element.54), channel_id=1, source_target_pairs={{0,24},{4,28},{8,0},{12,4},{16,8},{20,12},{24,16},{28,20},{1,25},{... | collective-permute-start | bytes 786440 | tf_op jit(solution)/shard_map/ppermute | solution.py:300
  76.0 21.6 %copy-start.4 = (bf16[2,128,512]{2,1,0:T(8,128)(2,1)S(1)}, bf16[2,128,512]{2,1,0:T(8,128)(2,1)}, u32[]{:S(2)}) copy-start(bf16[2,128,512]{2,1,0:T(8,128)(2,1)} %get-tuple-element.49) | copy-start | bytes 786436
  76.0 26.8 %copy-start.3 = (bf16[2,128,512]{2,1,0:T(8,128)(2,1)S(1)}, bf16[2,128,512]{2,1,0:T(8,128)(2,1)}, u32[]{:S(2)}) copy-start(bf16[2,128,512]{2,1,0:T(8,128)(2,1)} %get-tuple-element.55) | copy-start | bytes 786436
  76.0 43.6 %copy-start.1 = (f32[2,128,512]{2,1,0:T(8,128)S(1)}, f32[2,128,512]{2,1,0:T(8,128)}, u32[]{:S(2)}) copy-start(f32[2,128,512]{2,1,0:T(8,128)} %get-tuple-element.48) | copy-start | bytes 1572868
  97.6 31.7 %copy-start = (f32[2,512,128]{2,1,0:T(8,128)S(1)}, f32[2,512,128]{2,1,0:T(8,128)}, u32[]{:S(2)}) copy-start(f32[2,512,128]{2,1,0:T(8,128)} %get-tuple-element.44) | copy-start | bytes 1572868
  97.7 22.0 %collective-permute-start.6 = (bf16[2,128,512]{2,1,0:T(8,128)(2,1)S(1)}, bf16[2,128,512]{2,1,0:T(8,128)(2,1)S(1)}, u32[]{:S(2)}, u32[]{:S(2)}) collective-permute-start(bf16[2,128,512]{2,1,0:T(8,128)(2,1)S(1)} %copy-done.4), channel_id=1, source_target_pairs={{0,4},{4,8},{8,12},{12,16},{16,20},{20,24},{24,28},{28,0},{1,5},{5... | collective-permute-start | bytes 786440 | tf_op jit(solution)/shard_map/ppermute | solution.py:300
  102.8 16.8 %collective-permute-start.12 = (bf16[2,128,512]{2,1,0:T(8,128)(2,1)S(1)}, bf16[2,128,512]{2,1,0:T(8,128)(2,1)S(1)}, u32[]{:S(2)}, u32[]{:S(2)}) collective-permute-start(bf16[2,128,512]{2,1,0:T(8,128)(2,1)S(1)} %copy-done.3), channel_id=1, source_target_pairs={{0,28},{4,0},{8,4},{12,8},{16,12},{20,16},{24,20},{28,24},{1,29},{... | collective-permute-start | bytes 786440 | tf_op jit(solution)/shard_map/ppermute | solution.py:300
  109.4 11.5 %collective-permute-start.3 = (bf16[2,512,128]{2,1,0:T(8,128)(2,1)}, bf16[2,512,128]{2,1,0:T(8,128)(2,1)S(1)}, u32[]{:S(2)}, u32[]{:S(2)}) collective-permute-start(bf16[2,512,128]{2,1,0:T(8,128)(2,1)} %get-tuple-element.45), channel_id=1, source_target_pairs={{0,1},{1,2},{2,3},{3,0},{4,5},{5,6},{6,7},{7,4},{8,9},{9,10},{10,1... | collective-permute-start | bytes 786440 | tf_op jit(solution)/shard_map/ppermute | solution.py:300
  117.1 8.8 %collective-permute-start.4 = (bf16[2,512,128]{2,1,0:T(8,128)(2,1)}, bf16[2,512,128]{2,1,0:T(8,128)(2,1)S(1)}, u32[]{:S(2)}, u32[]{:S(2)}) collective-permute-start(bf16[2,512,128]{2,1,0:T(8,128)(2,1)} %get-tuple-element.46), channel_id=1, source_target_pairs={{0,2},{1,3},{2,0},{3,1},{4,6},{5,7},{6,4},{7,5},{8,10},{9,11},{10,... | collective-permute-start | bytes 786440 | tf_op jit(solution)/shard_map/ppermute | solution.py:300
  118.9 10.5 %collective-permute-start.5 = (bf16[2,512,128]{2,1,0:T(8,128)(2,1)}, bf16[2,512,128]{2,1,0:T(8,128)(2,1)S(1)}, u32[]{:S(2)}, u32[]{:S(2)}) collective-permute-start(bf16[2,512,128]{2,1,0:T(8,128)(2,1)} %get-tuple-element.47), channel_id=1, source_target_pairs={{0,3},{1,0},{2,1},{3,2},{4,7},{5,4},{6,5},{7,6},{8,11},{9,8},{10,9... | collective-permute-start | bytes 786440 | tf_op jit(solution)/shard_map/ppermute | solution.py:300
Sparse Core Ops, SparseCore 0:
  10.1 47.6 all-gather.1
